TPU v7x, 32 devices: a whole 2x2x4 slice. The times are simulated.
32 devices in a mesh: src: 4 (over z), dst: 4 (over y, core), rel: 2 (over x).
Axes of the slice: x: 2, y: 2, z: 4, core: 2. Of those that a mesh axis runs over, the one named last changes fastest.
Arguments:
- features: bfloat16 [2048, 512], P(('src', 'dst')), may hold values from -6 to 6
- out_grad: bfloat16 [2048, 512], P(('dst', 'src')), may hold values from -6 to 6
- weights: bfloat16 [2, 512, 512], P('rel'), may hold values from -0.25 to 0.25
- tiles: bfloat16 [2, 64, 128, 128], P('rel', ('src', 'dst')), may hold values from 0 to 1.5, as said below
- tile_rows: int32 [2, 64], P('rel', ('src', 'dst')), may hold values from 0 to 3
- tile_cols: int32 [2, 64], P('rel', ('src', 'dst')), may hold values from 0 to 3
- tile_count: int32 [2, 16], P('rel', ('src', 'dst')), may hold values from 1 to 4, as said below
- degrees: int32 [2, 2048], P('rel', ('dst', 'src')), may hold values from 1 to 64
Outputs:
- feature_grad: bfloat16 [2048, 512], P(('src', 'dst'))
- weight_grad: float32 [2, 512, 512], P('rel')
Inputs may be any that keep to these rules, and one draw needn't show every extreme that they name: An edge weight where an edge exists, else 0; the live tiles of one pair of panels lie at distinct positions. `tile_count`: the live slots are the first ones; pair 0 of every relation is full.
All inputs are finite; a program needn't handle non-finite values.
Results may differ from a plain program's by a relative error of at most 0.0024.
Values may be sent and summed in bfloat16 or wider, within the bound.
A program may use at most 64 MiB of HBM per device.

v0:
```python
import jax
import jax.numpy as jnp
from jax import lax
from jax.sharding import PartitionSpec as P


def body(features, out_grad, weights, tiles, tile_rows, tile_cols, tile_count, degrees):
    tile_size = tiles.shape[-1]
    width = features.shape[1]
    rows_dev = features.shape[0]
    n_dst = lax.axis_size("dst")
    n_cols = rows_dev * n_dst // tile_size
    group_size = 4
    scaled = (out_grad.astype(jnp.float32) / degrees[0].astype(jnp.float32)[:, None]).astype(
        jnp.bfloat16
    )
    panel = lax.all_gather(scaled, "src", axis=0, tiled=True)
    blocks = panel.reshape(-1, tile_size, width)
    live_count = tile_count[0, 0]

    def add_group(index, total):
        start = index * group_size
        tile_group = lax.dynamic_slice_in_dim(tiles[0], start, group_size, 0)
        row_group = lax.dynamic_slice_in_dim(tile_rows[0], start, group_size, 0)
        col_group = lax.dynamic_slice_in_dim(tile_cols[0], start, group_size, 0)
        picked = jnp.take(blocks, row_group, axis=0)
        contrib = jnp.einsum("gij,gjd->gid", tile_group, picked, preferred_element_type=jnp.float32)
        valid = (start + jnp.arange(group_size, dtype=jnp.int32) < live_count).astype(jnp.float32)
        return total.at[col_group].add(contrib * valid[:, None, None])

    n_groups = (live_count + group_size - 1) // group_size
    empty = jnp.zeros((n_cols, tile_size, width), jnp.float32)
    summed = lax.fori_loop(0, n_groups, add_group, empty)
    partial_value = summed.reshape(n_cols * tile_size, width)
    reduced = lax.psum_scatter(partial_value, "dst", scatter_dimension=0, tiled=True)
    local_weight = jnp.dot(features.astype(jnp.float32).T, reduced, precision=lax.Precision.HIGHEST)
    weight_grad = lax.psum(local_weight, ("src", "dst"))
    weight_wide = weights[0].astype(jnp.float32)
    own_part = jnp.dot(reduced, weight_wide.T, precision=lax.Precision.HIGHEST)
    feature_grad = lax.psum(own_part, "rel").astype(jnp.bfloat16)
    return (feature_grad, weight_grad[None])


def solution(mesh):
    in_specs = (
        P(("src", "dst"), None),
        P(("dst", "src"), None),
        P("rel", None, None),
        P("rel", ("src", "dst"), None, None),
        P("rel", ("src", "dst")),
        P("rel", ("src", "dst")),
        P("rel", ("src", "dst")),
        P("rel", ("dst", "src")),
    )
    out_specs = (P(("src", "dst"), None), P("rel", None, None))
    return jax.shard_map(body, mesh=mesh, in_specs=in_specs, out_specs=out_specs, check_vma=False)
```

profile of v0, /device:TPU:1, one launch (start us, length us, event | category | flops | bytes accessed | tf_op | source)
XLA Modules:
  0.0 166.9 jit_solution(13848207372994721381)
XLA Ops:
  7.2 0.0 copy-start
  7.2 0.0 reduce-scatter.2.cloned.1.call-start
  7.9 0.6 copy-done.5
  8.6 0.7 copy-done.4
  9.3 1.0 divide_convert_fusion
  10.3 15.3 %all_gather.3 = bf16[512,512]{1,0:T(8,128)(2,1)S(1)} all-gather(bf16[128,512]{1,0:T(8,128)(2,1)S(1)} %divide_convert_fusion), channel_id=1, replica_groups=mesh['src'=4,'dst'=4,'rel'=2] {'src'}, dimensions={0}, use_global_device_ids=true | all-gather | bytes 655360 | tf_op jit(solution)/shard_map/all_gather | solution.py:17
  25.6 0.6 gather_fusion
  26.1 0.3 copy.13
  26.5 1.1 broadcast_in_dim.23
  27.6 4.3 %while.12 = (s32[]{:T(128)}, f32[4,128,512]{2,1,0:T(8,128)}, s32[]{:T(128)}, s32[1,4]{1,0:T(1,128)S(1)}, s32[1,4]{1,0:T(1,128)S(1)}, /*index=5*/bf16[4,128,512]{...) while((s32[]{:T(128)}, f32[4,128,512]{2,1,0:T(8,128)}, ...), condition=%wide.region_2.3_spmd, body=%wide.region_0.2_spmd.sunk | while | flops 67895344 | bytes 6947041 | solution.py:33
  27.6 0.7 compare_convert_fusion.2
  28.2 0.3 fusion.20
  28.6 0.3 copy.16
  28.9 3.0 %scatter_fusion = f32[4,128,512]{2,1,0:T(8,128)} fusion(f32[4,128,512]{2,1,0:T(8,128)} %get-tuple-element.196, s32[4]{0:T(128)S(1)} %fusion.19, f32[4,128,512]{2,1,0:T(8,128)S(1)} %copy.16), kind=kCustom, calls=%fused_computation.1.clone.1 | custom fusion | flops 262144 | bytes 3145744 | tf_op jit(solution)/shard_map/while/body/scatter-add | solution.py:29
  31.9 0.0 reduce-scatter.2.cloned.1.call-update
  31.9 0.0 all-reduce.3.cloned.1.call-start
  32.0 28.3 %reduce-scatter.2.cloned.1.call-done = f32[128,512]{1,0:T(8,128)} async-done(((f32[512,512]{1,0:T(8,128)}), f32[128,512]{1,0:T(8,128)}) %reduce-scatter.2.cloned.1.call-update) | async-done | bytes 262160 | tf_op jit(solution)/shard_map/reduce_scatter | solution.py:35
  60.3 2.5 %convolution_bitcast_fusion = f32[1,512,512]{1,2,0:T(8,128)} fusion(f32[128,512]{1,0:T(8,128)} %reduce-scatter.2.cloned.1.call-done, bf16[128,512]{1,0:T(8,128)(2,1)S(1)} %copy-done.3), kind=kOutput, calls=%fused_computation.14 | convolution fusion | flops 402653184 | bytes 1441792 | tf_op jit(solution)/shard_map/dot_general | solution.py:36
  62.8 0.0 all-reduce.3.cloned.1.call-update
  62.8 0.9 copy-done.2
  63.7 0.6 fusion.7
  64.4 10.3 %all-reduce.4 = bf16[128,512]{1,0:T(8,128)(2,1)} all-reduce(f32[128,512]{1,0:T(8,128)S(1)} %fusion.7), channel_id=1, replica_groups=mesh['src'=4,'dst'=4,'rel'=2] {'rel'}, use_global_device_ids=true, to_apply=%region_4.5 | all-reduce | flops 65536 | bytes 393216 | tf_op jit(solution)/shard_map/psum | solution.py:40
  74.7 82.8 %all-reduce.3.cloned.1.call-done = f32[1,512,512]{1,2,0:T(8,128)} async-done(((f32[1,512,512]{1,2,0:T(8,128)}), f32[1,512,512]{1,2,0:T(8,128)}) %all-reduce.3.cloned.1.call-update) | async-done | bytes 1048592 | tf_op jit(solution)/shard_map/psum | solution.py:37
  157.5 2.5 %copy.14 = f32[1,512,512]{2,1,0:T(8,128)} copy(f32[1,512,512]{1,2,0:T(8,128)} %all-reduce.3.cloned.1.call-done) | data formatting | bytes 2097152
  (14 shorter events, 0.0 us)
Async XLA Ops:
  7.2 55.7 %copy-start = (bf16[1,512,512]{2,1,0:T(8,128)(2,1)S(1)}, bf16[1,512,512]{2,1,0:T(8,128)(2,1)}, u32[]{:S(2)}) copy-start(bf16[1,512,512]{2,1,0:T(8,128)(2,1)} %param.12) | copy-start | bytes 1572868
  7.2 53.1 %reduce-scatter.2.cloned.1.call-start = ((), (), s32[]{:S(2)}) async-start(), calls=%async_computation.1 | async-start | bytes 1310720 | tf_op jit(solution)/shard_map/reduce_scatter | solution.py:35
  7.9 0.7 copy-start.5
  8.6 0.7 copy-start.4
  26.4 1.1 copy-start.1
  26.5 1.1 copy-start.6
  31.9 28.4 %copy-start.3 = (bf16[128,512]{1,0:T(8,128)(2,1)S(1)}, bf16[128,512]{1,0:T(8,128)(2,1)}, u32[]{:S(2)}) copy-start(bf16[128,512]{1,0:T(8,128)(2,1)} %param.10) | copy-start | bytes 393220
  31.9 125.6 %all-reduce.3.cloned.1.call-start = ((), (), s32[]{:S(2)}) async-start(), calls=%async_computation.2 | async-start | bytes 2097152 | tf_op jit(solution)/shard_map/psum | solution.py:37
  62.8 0.9 copy-start.2
Sparse Core Ops, SparseCore 0:
  32.0 28.1 reduce-scatter.1
  64.7 92.7 all-reduce.2
where the time goes:
time: 168 us; the launch traced here: 167 us
  waiting for transfers between devices  111 us (66%)
  blocking collectives  25.6 us (15%)
  between operations  14.8 us (9%)
  local copies, waits for them, and re-layouts  7.05 us (4%)
  other arithmetic  4.64 us (3%)
  matrix products  3.52 us (2%)
    psum x1, waiting for transfers between devices, body(): weight_grad = lax.psum(local_weight, ('src', 'dst'))  82.8 us
    reduce_scatter x1, waiting for transfers between devices, body(): lax.psum_scatter(partial_value, 'dst', scatter_dimension=0, tiled=True)  28.3 us
    all_gather x1, blocking collectives, body(): panel = lax.all_gather(scaled, 'src', axis=0, tiled=True)  15.3 us
    psum x1, blocking collectives, body(): feature_grad = lax.psum(own_part, 'rel').astype(jnp.bfloat16)  10.3 us
    unnamed x15, local copies, waits for them, and re-layouts  4.77 us
  transfers between devices with their start and end apart: 2, of which 2 were waited for; matrix products, arithmetic and copies ran while one was open for 0% of the time, Pallas kernels for 0%

commit v1 on v0

--- a/solution.py
+++ b/solution.py
@@ -1,7 +1,210 @@
 import jax
 import jax.numpy as jnp
 from jax import lax
+from jax.experimental import pallas as pl
+from jax.experimental.pallas import tpu as pltpu
 from jax.sharding import PartitionSpec as P
+
+MESH = pl.DeviceIdType.MESH
+B = 128
+F32, BF16 = jnp.float32, jnp.bfloat16
+
+
+def split_high_low(x):
+    high = x.astype(BF16)
+    return high, (x - high.astype(F32)).astype(BF16)
+
+
+def kernel(
+    feat_ref, grad_ref, weight_ref, tiles_ref, rows_ref, cols_ref, count_ref, deg_ref,
+    fgrad_ref, wgrad_ref,
+    own, scal, meta, feats, feats_t, dense, red, rows_f32, wpart, wrecv, final, mine, other,
+    a_send, a_recv, t_send, t_recv, f_send, f_recv, c_send, c_recv, d_send, d_recv,
+    z_send, z_recv, y_send, y_recv, k_send, k_recv, g_send, g_recv, r_send, r_recv, x_send, x_recv,
+):
+    s, d, r = lax.axis_index("src"), lax.axis_index("dst"), lax.axis_index("rel")
+    peer = (d, d + 1 - 2 * (d % 2), (d + 2) % 4, 3 - d)
+
+    def zpos(step):
+        return (s + step) % 4
+
+    def to(source, target, send, recv, **device):
+        return pltpu.make_async_remote_copy(
+            src_ref=source, dst_ref=target, send_sem=send, recv_sem=recv,
+            device_id=device, device_id_type=MESH,
+        )
+
+    barrier = pltpu.get_barrier_semaphore()
+    for j in (1, 2, 3):
+        pl.semaphore_signal(barrier, inc=1, device_id={"dst": peer[j]}, device_id_type=MESH)
+        pl.semaphore_signal(barrier, inc=1, device_id={"src": zpos(j)}, device_id_type=MESH)
+    pl.semaphore_signal(barrier, inc=1, device_id={"rel": 1 - r}, device_id_type=MESH)
+
+    deg = jnp.broadcast_to(deg_ref[...].astype(F32), (B, B)).T
+    for slab in range(4):
+        own[slab] = (grad_ref[:, slab * B : (slab + 1) * B].astype(F32) / deg).astype(BF16)
+    line = lax.broadcasted_iota(jnp.int32, (16, B), 0)
+    place = jnp.full((16, B), -1, jnp.int32)
+    for t in range(4):
+        meta[0, t * B : (t + 1) * B, :] = tiles_ref[t]
+        where_t = rows_ref[0, t] * 4 + cols_ref[0, t]
+        place = jnp.where((line == t) & (t < count_ref[0, 0]), where_t, place)
+    meta[0, 4 * B : 4 * B + 16, :] = place.astype(F32).astype(BF16)
+    feats[0] = feat_ref[...]
+    scal[s, 0] = own[d]
+
+    pl.semaphore_wait(barrier, 7)
+
+    sent = []
+
+    def go(copy):
+        copy.start()
+        sent.append(copy)
+        return copy
+
+    slabs = [
+        go(to(own.at[peer[j]], scal.at[s, j], a_send.at[j], a_recv.at[j], dst=peer[j]))
+        for j in (1, 2, 3)
+    ]
+    tile_y = go(to(meta.at[0], meta.at[2], t_send.at[2], t_recv.at[2], dst=peer[2]))
+    tile_k = go(to(meta.at[0], meta.at[1], t_send.at[1], t_recv.at[1], dst=peer[1]))
+    feat_y = go(to(feats.at[0], feats.at[2], f_send.at[2], f_recv.at[2], dst=peer[2]))
+    feat_k = go(to(feats.at[0], feats.at[1], f_send.at[1], f_recv.at[1], dst=peer[1]))
+    for copy in slabs:
+        copy.wait_recv()
+    gathers = [
+        go(to(scal.at[s], scal.at[s], c_send.at[j], c_recv.at[j], src=zpos(j)))
+        for j in (1, 2, 3)
+    ]
+
+    def densify(j):
+        for k in range(4):
+            for c in range(4):
+                total = None
+                for t in range(4):
+                    code = meta[j, 4 * B + t : 4 * B + t + 1, :].astype(F32)
+                    hit = jnp.where(code == (k * 4 + peer[c]).astype(F32), 1.0, 0.0).astype(BF16)
+                    term = meta[j, t * B : (t + 1) * B, :] * hit
+                    total = term if total is None else total + term
+                dense[k, c * B : (c + 1) * B, j * B : (j + 1) * B] = total
+
+    densify(0)
+    tile_k.wait_recv()
+    densify(1)
+    tile_y.wait_recv()
+    tile_g = go(to(meta.at[2], meta.at[3], t_send.at[3], t_recv.at[3], dst=peer[1]))
+    densify(2)
+    feat_y.wait_recv()
+    feat_g = go(to(feats.at[2], feats.at[3], f_send.at[3], f_recv.at[3], dst=peer[1]))
+    feat_k.wait_recv()
+    tile_g.wait_recv()
+    densify(3)
+    for j in range(3):
+        feats_t[:, j * B : (j + 1) * B] = feats[j].T
+    feat_g.wait_recv()
+    feats_t[:, 3 * B :] = feats[3].T
+
+    def block_sum(at):
+        return jnp.dot(dense[at], scal[at].reshape(4 * B, B), preferred_element_type=F32)
+
+    total = block_sum(s)
+    for j in (1, 3, 2):
+        gathers[j - 1].wait_recv()
+        total = total + block_sum(zpos(4 - j))
+    for c in range(4):
+        red[c] = total[c * B : (c + 1) * B]
+    rows_f32[d] = red[0]
+    rows = [
+        go(to(red.at[j], rows_f32.at[d], r_send.at[j], r_recv.at[j], dst=peer[j]))
+        for j in (1, 2, 3)
+    ]
+    high, low = split_high_low(total)
+    for c in range(4):
+        left = feats_t[c * B : (c + 1) * B, :]
+        wpart[c] = jnp.dot(left, high, preferred_element_type=F32) + jnp.dot(
+            left, low, preferred_element_type=F32
+        )
+    parts = [
+        go(to(wpart.at[zpos(j)], wrecv.at[j], d_send.at[j], d_recv.at[j], src=zpos(j)))
+        for j in (1, 2, 3)
+    ]
+    for copy in rows:
+        copy.wait_recv()
+    value = None
+    for c in range(4):
+        right = weight_ref[:, c * B : (c + 1) * B]
+        for part in split_high_low(rows_f32[c]):
+            term = lax.dot_general(part, right, (((1,), (1,)), ((), ())), preferred_element_type=F32)
+            value = term if value is None else value + term
+    mine[...] = value
+    swap = go(to(mine, other, x_send.at[0], x_recv.at[0], rel=1 - r))
+    block = wpart[s]
+    for copy in parts:
+        copy.wait_recv()
+    block = block + wrecv[1] + wrecv[2] + wrecv[3]
+    final[d, s] = block.astype(BF16)
+
+    along = [
+        go(to(final.at[d, s], final.at[d, s], z_send.at[j], z_recv.at[j], src=zpos(j)))
+        for j in (1, 2, 3)
+    ]
+    ys, ks, gs = [], [], []
+    order = (0, 1, 3, 2)
+    for j in order:
+        if j:
+            along[j - 1].wait_recv()
+        at = final.at[d, zpos(4 - j)]
+        ys.append(go(to(at, at, y_send.at[j], y_recv.at[j], dst=peer[2])))
+        ks.append(go(to(at, at, k_send.at[j], k_recv.at[j], dst=peer[1])))
+    for n, j in enumerate(order):
+        ys[n].wait_recv()
+        at = final.at[peer[2], zpos(4 - j)]
+        gs.append(go(to(at, at, g_send.at[j], g_recv.at[j], dst=peer[1])))
+    swap.wait_recv()
+    fgrad_ref[...] = (mine[...] + other[...]).astype(BF16)
+    for copy in ks + gs:
+        copy.wait_recv()
+    for slab in range(4):
+        for q in range(4):
+            wgrad_ref[q * B : (q + 1) * B, slab * B : (slab + 1) * B] = final[slab, q]
+    for copy in sent:
+        copy.wait_send()
+
+
+def fast_body(features, out_grad, weights, tiles, tile_rows, tile_cols, tile_count, degrees):
+    vmem = pl.BlockSpec(memory_space=pltpu.VMEM)
+    smem = pl.BlockSpec(memory_space=pltpu.SMEM)
+    sem = pltpu.SemaphoreType.DMA((4,))
+    fgrad, wgrad = pl.pallas_call(
+        kernel,
+        out_shape=(
+            jax.ShapeDtypeStruct((B, 4 * B), BF16),
+            jax.ShapeDtypeStruct((4 * B, 4 * B), BF16),
+        ),
+        in_specs=[vmem, vmem, vmem, vmem, smem, smem, smem, vmem],
+        out_specs=(vmem, vmem),
+        scratch_shapes=[
+            pltpu.VMEM((4, B, B), BF16),
+            pltpu.VMEM((4, 4, B, B), BF16),
+            pltpu.VMEM((4, 4 * B + 16, B), BF16),
+            pltpu.VMEM((4, B, 4 * B), BF16),
+            pltpu.VMEM((4 * B, 4 * B), BF16),
+            pltpu.VMEM((4, 4 * B, 4 * B), BF16),
+            pltpu.VMEM((4, B, B), F32),
+            pltpu.VMEM((4, B, B), F32),
+            pltpu.VMEM((4, B, B), F32),
+            pltpu.VMEM((4, B, B), F32),
+            pltpu.VMEM((4, 4, B, B), BF16),
+            pltpu.VMEM((B, 4 * B), F32),
+            pltpu.VMEM((B, 4 * B), F32),
+        ]
+        + [sem] * 22,
+        compiler_params=pltpu.CompilerParams(
+            collective_id=0, has_side_effects=True, vmem_limit_bytes=32 * 1024 * 1024
+        ),
+        cost_estimate=pl.CostEstimate(flops=10**9, bytes_accessed=4 * 10**6, transcendentals=0),
+    )(features, out_grad, weights[0], tiles[0], tile_rows, tile_cols, tile_count, degrees)
+    return fgrad, wgrad.astype(F32)[None]
 
 
 def body(features, out_grad, weights, tiles, tile_rows, tile_cols, tile_count, degrees):
@@ -53,4 +256,15 @@
         P("rel", ("dst", "src")),
     )
     out_specs = (P(("src", "dst"), None), P("rel", None, None))
-    return jax.shard_map(body, mesh=mesh, in_specs=in_specs, out_specs=out_specs, check_vma=False)
+    sizes = (mesh.shape["src"], mesh.shape["dst"], mesh.shape["rel"])
+
+    def run(*args):
+        features, tiles = args[0], args[3]
+        shapes = (features.shape, tiles.shape)
+        small = sizes == (4, 4, 2) and shapes == ((16 * B, 4 * B), (2, 64, B, B))
+        chosen = fast_body if small else body
+        return jax.shard_map(
+            chosen, mesh=mesh, in_specs=in_specs, out_specs=out_specs, check_vma=False
+        )(*args)
+
+    return run

time: 168 us -> 47.3 us (0.28)
  waiting for transfers between devices: 111 us -> 0 us
  Pallas kernels: 0 us -> 39.5 us
  blocking collectives: 25.6 us -> 0 us
  between operations: 14.8 us -> 1.32 us
  other arithmetic: 4.64 us -> 1.1 us
  matrix products: 3.52 us -> 0 us
  local copies, waits for them, and re-layouts: 7.05 us -> 5.07 us
    psum x1 -> x0, waiting for transfers between devices: 82.8 us -> none  [body(): weight_grad = lax.psum(local_weight, ('src', 'dst'))]
    pallas_call x0 -> x1, Pallas kernels: none -> 39.5 us  [fast_body(): pl.pallas_call(kernel, out_shape=(jax.ShapeDtypeStruct((B, 4 * B), BF16),...]
    reduce_scatter x1 -> x0, waiting for transfers between devices: 28.3 us -> none  [body(): lax.psum_scatter(partial_value, 'dst', scatter_dimension=0, tiled=True)]
    all_gather x1 -> x0, blocking collectives: 15.3 us -> none  [body(): panel = lax.all_gather(scaled, 'src', axis=0, tiled=True)]
    psum x1 -> x0, blocking collectives: 10.3 us -> none  [body(): feature_grad = lax.psum(own_part, 'rel').astype(jnp.bfloat16)]
    dot_general x3 -> x0, matrix products: 3.52 us -> none  [the longest x1 2.54 us: body(): jnp.dot(features.astype(jnp.float32).T, reduced, precision=lax.Precision....]
    scatter-add x1 -> x0, other arithmetic: 2.98 us -> none  [add_group(): return total.at[col_group].add(contrib * valid[:, None, None])]
  transfers between devices with their start and end apart: 2 -> 0, of which waited for: 2 -> 0; matrix products, arithmetic and copies ran while one was open for 0% -> 0% of each run, Pallas kernels for 0% -> 0%
where the time goes in v1:
time: 47.3 us; the launch traced here: 46.9 us
  Pallas kernels  39.5 us (84%)
  local copies, waits for them, and re-layouts  5.07 us (11%)
  between operations  1.32 us (3%)
  other arithmetic  1.1 us (2%)
    pallas_call x1, Pallas kernels, fast_body(): pl.pallas_call(kernel, out_shape=(jax.ShapeDtypeStruct((B, 4 * B), BF16),...  39.5 us
    unnamed x15, local copies, waits for them, and re-layouts  5.07 us
    broadcast_in_dim x1, other arithmetic, fast_body(): return (fgrad, wgrad.astype(F32)[None])  1.1 us

profile of v1, /device:TPU:1, one launch (start us, length us, event | category | flops | bytes accessed | tf_op | source)
XLA Modules:
  0.0 46.9 jit_solution(205534613716972920)
XLA Ops:
  1.3 0.0 copy-start.4
  1.3 0.0 copy-start.5
  1.3 0.0 copy-start.6
  1.3 0.6 %copy-done.4 = s32[1,4]{1,0:T(1,128)S(1)} copy-done((s32[1,4]{1,0:T(1,128)S(1)}, s32[1,4]{1,0:T(1,128)}, u32[]{:S(2)}) %copy-start.4) | copy-done | bytes 40
  1.9 0.0 copy-done.5
  2.0 0.0 copy-done.6
  2.0 0.0 copy-start
  2.0 1.0 %copy-done = bf16[1,512,512]{2,1,0:T(8,128)(2,1)S(1)} copy-done((bf16[1,512,512]{2,1,0:T(8,128)(2,1)S(1)}, bf16[1,512,512]{2,1,0:T(8,128)(2,1)}, u32[]{:S(2)}) %copy-start) | copy-done | bytes 524312
  3.0 0.0 copy-start.1
  3.0 0.9 %copy-done.1 = bf16[128,512]{1,0:T(8,128)(2,1)S(1)} copy-done((bf16[128,512]{1,0:T(8,128)(2,1)S(1)}, bf16[128,512]{1,0:T(8,128)(2,1)}, u32[]{:S(2)}) %copy-start.1) | copy-done | bytes 131096
  3.9 0.0 copy-start.2
  3.9 0.9 %copy-done.2 = bf16[128,512]{1,0:T(8,128)(2,1)S(1)} copy-done((bf16[128,512]{1,0:T(8,128)(2,1)S(1)}, bf16[128,512]{1,0:T(8,128)(2,1)}, u32[]{:S(2)}) %copy-start.2) | copy-done | bytes 131096
  4.8 0.0 copy-start.3
  4.8 0.9 %copy-done.3 = bf16[1,4,128,128]{3,2,1,0:T(8,128)(2,1)S(1)} copy-done((bf16[1,4,128,128]{3,2,1,0:T(8,128)(2,1)S(1)}, bf16[1,4,128,128]{3,2,1,0:T(8,128)(2,1)}, u32[]{:S(2)}) %copy-start.3) | copy-done | bytes 131096
  5.7 39.5 %shard_map.95 = (bf16[128,512]{1,0:T(8,128)(2,1)S(1)}, bf16[512,512]{1,0:T(8,128)(2,1)S(1)}) custom-call(bf16[128,512]{1,0:T(8,128)(2,1)S(1)} %copy-done.1, bf16[128,512]{1,0:T(8,128)(2,1)S(1)} %copy-done.2, bf16[512,512]{1,0:T(8,128)(2,1)S(1)} %bitcast.5, bf16[4,128,128]{2,1,0:T(8,128)(2,1)S(1)} %bitcast.6, s32[1,4]{1,0:T(1,128)S(1)} %copy-done.4, ...), custom_call_target="tpu_custom_call" | custom-call | flops 1000000000 | bytes 4000000 | tf_op jit(solution)/shard_map/pallas_call | solution.py:178
  45.2 1.1 %bitcast_convert_fusion = f32[1,512,512]{2,1,0:T(8,128)} fusion(bf16[512,512]{1,0:T(8,128)(2,1)S(1)} %get-tuple-element.5), kind=kLoop, calls=%fused_computation | loop fusion | flops 262144 | bytes 1572864 | tf_op jit(solution)/shard_map/broadcast_in_dim | solution.py:207
  46.3 0.7 %copy.12 = bf16[128,512]{1,0:T(8,128)(2,1)} copy(bf16[128,512]{1,0:T(8,128)(2,1)S(1)} %get-tuple-element.8) | data formatting | bytes 262144
Async XLA Ops:
  1.3 0.7 %copy-start.4 = (s32[1,4]{1,0:T(1,128)S(1)}, s32[1,4]{1,0:T(1,128)}, u32[]{:S(2)}) copy-start(s32[1,4]{1,0:T(1,128)} %rows_ref.1) | copy-start | bytes 52
  1.3 0.7 %copy-start.5 = (s32[1,4]{1,0:T(1,128)S(1)}, s32[1,4]{1,0:T(1,128)}, u32[]{:S(2)}) copy-start(s32[1,4]{1,0:T(1,128)} %cols_ref.1) | copy-start | bytes 52
  1.3 0.7 %copy-start.6 = (s32[1,128]{1,0:T(1,128)S(1)}, s32[1,128]{1,0:T(1,128)}, u32[]{:S(2)}) copy-start(s32[1,128]{1,0:T(1,128)} %deg_ref.1) | copy-start | bytes 1540
  2.0 1.0 %copy-start = (bf16[1,512,512]{2,1,0:T(8,128)(2,1)S(1)}, bf16[1,512,512]{2,1,0:T(8,128)(2,1)}, u32[]{:S(2)}) copy-start(bf16[1,512,512]{2,1,0:T(8,128)(2,1)} %param.10) | copy-start | bytes 1572868
  3.0 0.9 %copy-start.1 = (bf16[128,512]{1,0:T(8,128)(2,1)S(1)}, bf16[128,512]{1,0:T(8,128)(2,1)}, u32[]{:S(2)}) copy-start(bf16[128,512]{1,0:T(8,128)(2,1)} %feat_ref.1) | copy-start | bytes 393220
  3.9 0.9 %copy-start.2 = (bf16[128,512]{1,0:T(8,128)(2,1)S(1)}, bf16[128,512]{1,0:T(8,128)(2,1)}, u32[]{:S(2)}) copy-start(bf16[128,512]{1,0:T(8,128)(2,1)} %grad_ref.1) | copy-start | bytes 393220
  4.8 0.9 %copy-start.3 = (bf16[1,4,128,128]{3,2,1,0:T(8,128)(2,1)S(1)}, bf16[1,4,128,128]{3,2,1,0:T(8,128)(2,1)}, u32[]{:S(2)}) copy-start(bf16[1,4,128,128]{3,2,1,0:T(8,128)(2,1)} %param.11) | copy-start | bytes 393220

commit v2 on v1

--- a/solution.py
+++ b/solution.py
@@ -18,8 +18,8 @@
 def kernel(
     feat_ref, grad_ref, weight_ref, tiles_ref, rows_ref, cols_ref, count_ref, deg_ref,
     fgrad_ref, wgrad_ref,
-    own, scal, meta, feats, feats_t, dense, red, rows_f32, wpart, wrecv, final, mine, other,
-    a_send, a_recv, t_send, t_recv, f_send, f_recv, c_send, c_recv, d_send, d_recv,
+    grad, weight, deg_in, rows_in, cols_in, count_in, total, own, scal, meta, feats, feats_t, dense, red, rows_f32, wpart, wrecv, final, mine, other,
+    l_sem, right_send, left_send, c_recv, a_send, a_recv, t_send, t_recv, f_send, f_recv, d_send, d_recv,
     z_send, z_recv, y_send, y_recv, k_send, k_recv, g_send, g_recv, r_send, r_recv, x_send, x_recv,
 ):
     s, d, r = lax.axis_index("src"), lax.axis_index("dst"), lax.axis_index("rel")
@@ -34,24 +34,38 @@
             device_id=device, device_id_type=MESH,
         )
 
+    loads = [
+        pltpu.make_async_copy(source, target, l_sem.at[n])
+        for n, (source, target) in enumerate((
+            (grad_ref, grad), (deg_ref, deg_in), (rows_ref, rows_in), (cols_ref, cols_in),
+            (count_ref, count_in), (tiles_ref, meta.at[0, pl.ds(0, 4 * B)]),
+            (feat_ref, feats.at[0]), (weight_ref, weight),
+        ))
+    ]
+    for copy in loads:
+        copy.start()
     barrier = pltpu.get_barrier_semaphore()
     for j in (1, 2, 3):
         pl.semaphore_signal(barrier, inc=1, device_id={"dst": peer[j]}, device_id_type=MESH)
         pl.semaphore_signal(barrier, inc=1, device_id={"src": zpos(j)}, device_id_type=MESH)
     pl.semaphore_signal(barrier, inc=1, device_id={"rel": 1 - r}, device_id_type=MESH)
 
-    deg = jnp.broadcast_to(deg_ref[...].astype(F32), (B, B)).T
+    loads[0].wait()
+    loads[1].wait()
+    deg = jnp.broadcast_to(deg_in[...].astype(F32), (B, B)).T
     for slab in range(4):
-        own[slab] = (grad_ref[:, slab * B : (slab + 1) * B].astype(F32) / deg).astype(BF16)
+        own[slab] = (grad[:, slab * B : (slab + 1) * B].astype(F32) / deg).astype(BF16)
+    for n in (2, 3, 4):
+        loads[n].wait()
     line = lax.broadcasted_iota(jnp.int32, (16, B), 0)
     place = jnp.full((16, B), -1, jnp.int32)
     for t in range(4):
-        meta[0, t * B : (t + 1) * B, :] = tiles_ref[t]
-        where_t = rows_ref[0, t] * 4 + cols_ref[0, t]
-        place = jnp.where((line == t) & (t < count_ref[0, 0]), where_t, place)
+        where_t = rows_in[0, t] * 4 + cols_in[0, t]
+        place = jnp.where((line == t) & (t < count_in[0, 0]), where_t, place)
     meta[0, 4 * B : 4 * B + 16, :] = place.astype(F32).astype(BF16)
-    feats[0] = feat_ref[...]
     scal[s, 0] = own[d]
+    loads[5].wait()
+    loads[6].wait()
 
     pl.semaphore_wait(barrier, 7)
 
@@ -62,20 +76,54 @@
         sent.append(copy)
         return copy
 
-    slabs = [
+    def chain(at, j, right):
+        return to(
+            scal.at[at, j], scal.at[at, j], (right_send if right else left_send).at[at, j],
+            c_recv.at[at, j], src=zpos(1 if right else 3),
+        )
+
+    def push(j):
+        @pl.when(s < 3)
+        def _():
+            chain(s, j, True).start()
+
+        @pl.when(s > 0)
+        def _():
+            chain(s, j, False).start()
+
+    def forward(n):
+        for j in range(4):
+            @pl.when(s >= n)
+            def _():
+                chain(zpos(4 - n), j, True).wait_recv()
+
+            @pl.when((s >= n) & (s < 3))
+            def _():
+                chain(zpos(4 - n), j, True).start()
+
+            @pl.when(s + n <= 3)
+            def _():
+                chain(zpos(n), j, False).wait_recv()
+
+            @pl.when((s + n <= 3) & (s > 0))
+            def _():
+                chain(zpos(n), j, False).start()
+
+    slab_y, slab_g, slab_k = [
         go(to(own.at[peer[j]], scal.at[s, j], a_send.at[j], a_recv.at[j], dst=peer[j]))
-        for j in (1, 2, 3)
+        for j in (2, 3, 1)
     ]
+    push(0)
     tile_y = go(to(meta.at[0], meta.at[2], t_send.at[2], t_recv.at[2], dst=peer[2]))
     tile_k = go(to(meta.at[0], meta.at[1], t_send.at[1], t_recv.at[1], dst=peer[1]))
     feat_y = go(to(feats.at[0], feats.at[2], f_send.at[2], f_recv.at[2], dst=peer[2]))
     feat_k = go(to(feats.at[0], feats.at[1], f_send.at[1], f_recv.at[1], dst=peer[1]))
-    for copy in slabs:
-        copy.wait_recv()
-    gathers = [
-        go(to(scal.at[s], scal.at[s], c_send.at[j], c_recv.at[j], src=zpos(j)))
-        for j in (1, 2, 3)
-    ]
+    slab_k.wait_recv()
+    push(1)
+    slab_y.wait_recv()
+    push(2)
+    slab_g.wait_recv()
+    push(3)
 
     def densify(j):
         for k in range(4):
@@ -88,59 +136,71 @@
                     total = term if total is None else total + term
                 dense[k, c * B : (c + 1) * B, j * B : (j + 1) * B] = total
 
+    def add(at):
+        total[...] += jnp.dot(dense[at], scal[at].reshape(4 * B, B), preferred_element_type=F32)
+
+    def add_all(n):
+        @pl.when(s >= n)
+        def _():
+            add(zpos(4 - n))
+
+        @pl.when(s + n <= 3)
+        def _():
+            add(zpos(n))
+
     densify(0)
     tile_k.wait_recv()
     densify(1)
+    forward(1)
     tile_y.wait_recv()
     tile_g = go(to(meta.at[2], meta.at[3], t_send.at[3], t_recv.at[3], dst=peer[1]))
     densify(2)
+    forward(2)
+    tile_g.wait_recv()
+    densify(3)
     feat_y.wait_recv()
     feat_g = go(to(feats.at[2], feats.at[3], f_send.at[3], f_recv.at[3], dst=peer[1]))
     feat_k.wait_recv()
-    tile_g.wait_recv()
-    densify(3)
     for j in range(3):
-        feats_t[:, j * B : (j + 1) * B] = feats[j].T
+        feats_t[:, :, j * B : (j + 1) * B] = feats[j].T.reshape(4, B, B)
+    total[...] = jnp.zeros((4 * B, B), F32)
+    add(s)
+    add_all(1)
+    add_all(2)
     feat_g.wait_recv()
-    feats_t[:, 3 * B :] = feats[3].T
-
-    def block_sum(at):
-        return jnp.dot(dense[at], scal[at].reshape(4 * B, B), preferred_element_type=F32)
-
-    total = block_sum(s)
-    for j in (1, 3, 2):
-        gathers[j - 1].wait_recv()
-        total = total + block_sum(zpos(4 - j))
+    feats_t[:, :, 3 * B :] = feats[3].T.reshape(4, B, B)
+    forward(3)
+    add_all(3)
     for c in range(4):
-        red[c] = total[c * B : (c + 1) * B]
+        red[c] = total[c * B : (c + 1) * B, :]
     rows_f32[d] = red[0]
     rows = [
         go(to(red.at[j], rows_f32.at[d], r_send.at[j], r_recv.at[j], dst=peer[j]))
         for j in (1, 2, 3)
     ]
-    high, low = split_high_low(total)
-    for c in range(4):
-        left = feats_t[c * B : (c + 1) * B, :]
-        wpart[c] = jnp.dot(left, high, preferred_element_type=F32) + jnp.dot(
+    high, low = split_high_low(total[...])
+    parts = {}
+    for j in (2, 1, 3, 0):
+        left = feats_t[zpos(j)]
+        wpart[j] = jnp.dot(left, high, preferred_element_type=F32) + jnp.dot(
             left, low, preferred_element_type=F32
         )
-    parts = [
-        go(to(wpart.at[zpos(j)], wrecv.at[j], d_send.at[j], d_recv.at[j], src=zpos(j)))
-        for j in (1, 2, 3)
-    ]
+        if j:
+            parts[j] = go(to(wpart.at[j], wrecv.at[j], d_send.at[j], d_recv.at[j], src=zpos(j)))
     for copy in rows:
         copy.wait_recv()
+    loads[7].wait()
     value = None
     for c in range(4):
-        right = weight_ref[:, c * B : (c + 1) * B]
+        right = weight[:, c * B : (c + 1) * B]
         for part in split_high_low(rows_f32[c]):
             term = lax.dot_general(part, right, (((1,), (1,)), ((), ())), preferred_element_type=F32)
             value = term if value is None else value + term
     mine[...] = value
     swap = go(to(mine, other, x_send.at[0], x_recv.at[0], rel=1 - r))
-    block = wpart[s]
-    for copy in parts:
-        copy.wait_recv()
+    block = wpart[0]
+    for j in (1, 3, 2):
+        parts[j].wait_recv()
     block = block + wrecv[1] + wrecv[2] + wrecv[3]
     final[d, s] = block.astype(BF16)
 
@@ -169,11 +229,19 @@
             wgrad_ref[q * B : (q + 1) * B, slab * B : (slab + 1) * B] = final[slab, q]
     for copy in sent:
         copy.wait_send()
+    for n in range(3):
+        for j in range(4):
+            @pl.when((s >= n) & (s < 3))
+            def _():
+                chain(zpos(4 - n), j, True).wait_send()
+
+            @pl.when((s + n <= 3) & (s > 0))
+            def _():
+                chain(zpos(n), j, False).wait_send()
 
 
 def fast_body(features, out_grad, weights, tiles, tile_rows, tile_cols, tile_count, degrees):
     vmem = pl.BlockSpec(memory_space=pltpu.VMEM)
-    smem = pl.BlockSpec(memory_space=pltpu.SMEM)
     sem = pltpu.SemaphoreType.DMA((4,))
     fgrad, wgrad = pl.pallas_call(
         kernel,
@@ -181,14 +249,21 @@
             jax.ShapeDtypeStruct((B, 4 * B), BF16),
             jax.ShapeDtypeStruct((4 * B, 4 * B), BF16),
         ),
-        in_specs=[vmem, vmem, vmem, vmem, smem, smem, smem, vmem],
+        in_specs=[pl.BlockSpec(memory_space=pl.ANY)] * 8,
         out_specs=(vmem, vmem),
         scratch_shapes=[
+            pltpu.VMEM((B, 4 * B), BF16),
+            pltpu.VMEM((4 * B, 4 * B), BF16),
+            pltpu.VMEM((1, B), jnp.int32),
+            pltpu.SMEM((1, 4), jnp.int32),
+            pltpu.SMEM((1, 4), jnp.int32),
+            pltpu.SMEM((1, 1), jnp.int32),
+            pltpu.VMEM((4 * B, B), F32),
             pltpu.VMEM((4, B, B), BF16),
             pltpu.VMEM((4, 4, B, B), BF16),
             pltpu.VMEM((4, 4 * B + 16, B), BF16),
             pltpu.VMEM((4, B, 4 * B), BF16),
-            pltpu.VMEM((4 * B, 4 * B), BF16),
+            pltpu.VMEM((4, B, 4 * B), BF16),
             pltpu.VMEM((4, 4 * B, 4 * B), BF16),
             pltpu.VMEM((4, B, B), F32),
             pltpu.VMEM((4, B, B), F32),
@@ -198,12 +273,14 @@
             pltpu.VMEM((B, 4 * B), F32),
             pltpu.VMEM((B, 4 * B), F32),
         ]
-        + [sem] * 22,
+        + [pltpu.SemaphoreType.DMA((8,))]
+        + [pltpu.SemaphoreType.DMA((4, 4))] * 3
+        + [sem] * 20,
         compiler_params=pltpu.CompilerParams(
-            collective_id=0, has_side_effects=True, vmem_limit_bytes=32 * 1024 * 1024
+            collective_id=0, has_side_effects=True, vmem_limit_bytes=56 * 1024 * 1024
         ),
         cost_estimate=pl.CostEstimate(flops=10**9, bytes_accessed=4 * 10**6, transcendentals=0),
-    )(features, out_grad, weights[0], tiles[0], tile_rows, tile_cols, tile_count, degrees)
+    )(features, out_grad, weights[0], tiles[0].reshape(4 * B, B), tile_rows, tile_cols, tile_count, degrees)
     return fgrad, wgrad.astype(F32)[None]
 
 

time: 47.3 us -> 39.4 us (0.83)
  local copies, waits for them, and re-layouts: 5.07 us -> 0.66 us
  Pallas kernels: 39.5 us -> 35.1 us
  other arithmetic: 1.1 us -> 2.18 us
    unnamed x15 -> x3, local copies, waits for them, and re-layouts: 5.07 us -> 0.66 us
    pallas_call x1, Pallas kernels: 39.5 us -> 35.1 us  [fast_body(): pl.pallas_call(kernel, out_shape=(jax.ShapeDtypeStruct((B, 4 * B), BF16),...]
    broadcast_in_dim x1, other arithmetic: 1.1 us -> 2.18 us  [fast_body(): return (fgrad, wgrad.astype(F32)[None])]
where the time goes in v2:
time: 39.4 us; the launch traced here: 39.2 us
  Pallas kernels  35.1 us (89%)
  other arithmetic  2.18 us (6%)
  between operations  1.3 us (3%)
  local copies, waits for them, and re-layouts  0.66 us (2%)
    pallas_call x1, Pallas kernels, fast_body(): pl.pallas_call(kernel, out_shape=(jax.ShapeDtypeStruct((B, 4 * B), BF16),...  35.1 us
    broadcast_in_dim x1, other arithmetic, fast_body(): return (fgrad, wgrad.astype(F32)[None])  2.18 us

profile of v2, /device:TPU:1, one launch (start us, length us, event | category | flops | bytes accessed | tf_op | source)
XLA Modules:
  0.0 39.2 jit_solution(16413159135935666418)
XLA Ops:
  1.3 35.1 %shard_map.95 = (bf16[128,512]{1,0:T(8,128)(2,1)}, bf16[512,512]{1,0:T(8,128)(2,1)}) custom-call(bf16[128,512]{1,0:T(8,128)(2,1)} %feat_ref.1, bf16[128,512]{1,0:T(8,128)(2,1)} %grad_ref.1, bf16[512,512]{1,0:T(8,128)(2,1)} %bitcast.5, bf16[512,128]{1,0:T(8,128)(2,1)} %bitcast.6, s32[1,4]{1,0:T(1,128)} %rows_ref.1, s32[1,4]{1,0:T(1,128)} %cols_ref.1, ...), custom_call_target="tpu_custom_call" | custom-call | flops 1000000000 | bytes 4000000 | tf_op jit(solution)/shard_map/pallas_call | solution.py:246
  36.4 0.0 copy-start
  36.4 2.2 %bitcast_convert_fusion = f32[1,512,512]{2,1,0:T(8,128)} fusion(bf16[512,512]{1,0:T(8,128)(2,1)} %get-tuple-element.5), kind=kLoop, calls=%fused_computation | loop fusion | flops 262144 | bytes 1572864 | tf_op jit(solution)/shard_map/broadcast_in_dim | solution.py:284
  38.5 0.0 copy-done
  38.6 0.7 %copy.12 = bf16[128,512]{1,0:T(8,128)(2,1)} copy(bf16[128,512]{1,0:T(8,128)(2,1)S(1)} %copy-done) | data formatting | bytes 262144
Async XLA Ops:
  36.4 2.2 %copy-start = (bf16[128,512]{1,0:T(8,128)(2,1)S(1)}, bf16[128,512]{1,0:T(8,128)(2,1)}, u32[]{:S(2)}) copy-start(bf16[128,512]{1,0:T(8,128)(2,1)} %get-tuple-element.8) | copy-start | bytes 393220

commit v3 on v2

--- a/solution.py
+++ b/solution.py
@@ -7,6 +7,7 @@
 
 MESH = pl.DeviceIdType.MESH
 B = 128
+HALF = B // 2
 F32, BF16 = jnp.float32, jnp.bfloat16
 
 
@@ -47,8 +48,15 @@
     barrier = pltpu.get_barrier_semaphore()
     for j in (1, 2, 3):
         pl.semaphore_signal(barrier, inc=1, device_id={"dst": peer[j]}, device_id_type=MESH)
-        pl.semaphore_signal(barrier, inc=1, device_id={"src": zpos(j)}, device_id_type=MESH)
     pl.semaphore_signal(barrier, inc=1, device_id={"rel": 1 - r}, device_id_type=MESH)
+
+    @pl.when(s < 3)
+    def _():
+        pl.semaphore_signal(barrier, inc=1, device_id={"src": zpos(1)}, device_id_type=MESH)
+
+    @pl.when(s > 0)
+    def _():
+        pl.semaphore_signal(barrier, inc=1, device_id={"src": zpos(3)}, device_id_type=MESH)
 
     loads[0].wait()
     loads[1].wait()
@@ -67,7 +75,18 @@
     loads[5].wait()
     loads[6].wait()
 
-    pl.semaphore_wait(barrier, 7)
+    pl.semaphore_wait(barrier, 4 + (s + 3) // 4 + (6 - s) // 4)
+
+    def densify(j):
+        for k in range(4):
+            for c in range(4):
+                total = None
+                for t in range(4):
+                    code = meta[j, 4 * B + t : 4 * B + t + 1, :].astype(F32)
+                    hit = jnp.where(code == (k * 4 + peer[c]).astype(F32), 1.0, 0.0).astype(BF16)
+                    term = meta[j, t * B : (t + 1) * B, :] * hit
+                    total = term if total is None else total + term
+                dense[k, c * B : (c + 1) * B, j * B : (j + 1) * B] = total
 
     sent = []
 
@@ -91,8 +110,8 @@
         def _():
             chain(s, j, False).start()
 
-    def forward(n):
-        for j in range(4):
+    def forward(n, *js):
+        for j in js:
             @pl.when(s >= n)
             def _():
                 chain(zpos(4 - n), j, True).wait_recv()
@@ -120,22 +139,12 @@
     feat_k = go(to(feats.at[0], feats.at[1], f_send.at[1], f_recv.at[1], dst=peer[1]))
     slab_k.wait_recv()
     push(1)
+    densify(0)
     slab_y.wait_recv()
     push(2)
     slab_g.wait_recv()
     push(3)
 
-    def densify(j):
-        for k in range(4):
-            for c in range(4):
-                total = None
-                for t in range(4):
-                    code = meta[j, 4 * B + t : 4 * B + t + 1, :].astype(F32)
-                    hit = jnp.where(code == (k * 4 + peer[c]).astype(F32), 1.0, 0.0).astype(BF16)
-                    term = meta[j, t * B : (t + 1) * B, :] * hit
-                    total = term if total is None else total + term
-                dense[k, c * B : (c + 1) * B, j * B : (j + 1) * B] = total
-
     def add(at):
         total[...] += jnp.dot(dense[at], scal[at].reshape(4 * B, B), preferred_element_type=F32)
 
@@ -148,14 +157,14 @@
         def _():
             add(zpos(n))
 
-    densify(0)
+    forward(1, 0, 1)
     tile_k.wait_recv()
     densify(1)
-    forward(1)
+    forward(1, 2, 3)
     tile_y.wait_recv()
     tile_g = go(to(meta.at[2], meta.at[3], t_send.at[3], t_recv.at[3], dst=peer[1]))
     densify(2)
-    forward(2)
+    forward(2, 0, 1, 2, 3)
     tile_g.wait_recv()
     densify(3)
     feat_y.wait_recv()
@@ -169,7 +178,7 @@
     add_all(2)
     feat_g.wait_recv()
     feats_t[:, :, 3 * B :] = feats[3].T.reshape(4, B, B)
-    forward(3)
+    forward(3, 0, 1, 2, 3)
     add_all(3)
     for c in range(4):
         red[c] = total[c * B : (c + 1) * B, :]
@@ -180,13 +189,22 @@
     ]
     high, low = split_high_low(total[...])
     parts = {}
+
+    def part(j, h):
+        at = pl.ds(h * HALF, HALF)
+        return to(
+            wpart.at[j, at], wrecv.at[j, at], d_send.at[j, h], d_recv.at[j, h], src=zpos(j)
+        )
+
     for j in (2, 1, 3, 0):
         left = feats_t[zpos(j)]
         wpart[j] = jnp.dot(left, high, preferred_element_type=F32) + jnp.dot(
             left, low, preferred_element_type=F32
         )
         if j:
-            parts[j] = go(to(wpart.at[j], wrecv.at[j], d_send.at[j], d_recv.at[j], src=zpos(j)))
+            parts[j, 0] = go(part(j, 0))
+    for j in (2, 1, 3):
+        parts[j, 1] = go(part(j, 1))
     for copy in rows:
         copy.wait_recv()
     loads[7].wait()
@@ -198,35 +216,45 @@
             value = term if value is None else value + term
     mine[...] = value
     swap = go(to(mine, other, x_send.at[0], x_recv.at[0], rel=1 - r))
-    block = wpart[0]
-    for j in (1, 3, 2):
-        parts[j].wait_recv()
-    block = block + wrecv[1] + wrecv[2] + wrecv[3]
-    final[d, s] = block.astype(BF16)
-
-    along = [
-        go(to(final.at[d, s], final.at[d, s], z_send.at[j], z_recv.at[j], src=zpos(j)))
-        for j in (1, 2, 3)
-    ]
-    ys, ks, gs = [], [], []
     order = (0, 1, 3, 2)
+    along, ys, ks, gs = {}, {}, {}, {}
+
+    def pass_on(j, h):
+        at = final.at[d, zpos(4 - j), h]
+        ys[j, h] = go(to(at, at, y_send.at[j, h], y_recv.at[j, h], dst=peer[2]))
+        ks[j, h] = go(to(at, at, k_send.at[j, h], k_recv.at[j, h], dst=peer[1]))
+
+    for h in range(2):
+        rows_h = slice(h * HALF, (h + 1) * HALF)
+        block = wpart[0, rows_h]
+        for j in (1, 3, 2):
+            parts[j, h].wait_recv()
+        block = block + wrecv[1, rows_h] + wrecv[2, rows_h] + wrecv[3, rows_h]
+        final[d, s, h] = block.astype(BF16)
+        at = final.at[d, s, h]
+        for j in (2, 1, 3):
+            along[j, h] = go(to(at, at, z_send.at[j, h], z_recv.at[j, h], src=zpos(j)))
+        pass_on(0, h)
+    for h in range(2):
+        for j in order:
+            if j:
+                along[j, h].wait_recv()
+                pass_on(j, h)
+            if h == 1:
+                ys[j, 0].wait_recv()
+                at = final.at[peer[2], zpos(4 - j), 0]
+                gs[j, 0] = go(to(at, at, g_send.at[j, 0], g_recv.at[j, 0], dst=peer[1]))
     for j in order:
-        if j:
-            along[j - 1].wait_recv()
-        at = final.at[d, zpos(4 - j)]
-        ys.append(go(to(at, at, y_send.at[j], y_recv.at[j], dst=peer[2])))
-        ks.append(go(to(at, at, k_send.at[j], k_recv.at[j], dst=peer[1])))
-    for n, j in enumerate(order):
-        ys[n].wait_recv()
-        at = final.at[peer[2], zpos(4 - j)]
-        gs.append(go(to(at, at, g_send.at[j], g_recv.at[j], dst=peer[1])))
+        ys[j, 1].wait_recv()
+        at = final.at[peer[2], zpos(4 - j), 1]
+        gs[j, 1] = go(to(at, at, g_send.at[j, 1], g_recv.at[j, 1], dst=peer[1]))
     swap.wait_recv()
     fgrad_ref[...] = (mine[...] + other[...]).astype(BF16)
-    for copy in ks + gs:
+    for copy in [*ks.values(), *gs.values()]:
         copy.wait_recv()
     for slab in range(4):
         for q in range(4):
-            wgrad_ref[q * B : (q + 1) * B, slab * B : (slab + 1) * B] = final[slab, q]
+            wgrad_ref[q * B : (q + 1) * B, slab * B : (slab + 1) * B] = final[slab, q].reshape(B, B)
     for copy in sent:
         copy.wait_send()
     for n in range(3):
@@ -269,13 +297,15 @@
             pltpu.VMEM((4, B, B), F32),
             pltpu.VMEM((4, B, B), F32),
             pltpu.VMEM((4, B, B), F32),
-            pltpu.VMEM((4, 4, B, B), BF16),
+            pltpu.VMEM((4, 4, 2, HALF, B), BF16),
             pltpu.VMEM((B, 4 * B), F32),
             pltpu.VMEM((B, 4 * B), F32),
         ]
         + [pltpu.SemaphoreType.DMA((8,))]
         + [pltpu.SemaphoreType.DMA((4, 4))] * 3
-        + [sem] * 20,
+        + [sem] * 6
+        + [pltpu.SemaphoreType.DMA((4, 2))] * 10
+        + [sem] * 4,
         compiler_params=pltpu.CompilerParams(
             collective_id=0, has_side_effects=True, vmem_limit_bytes=56 * 1024 * 1024
         ),

time: 39.4 us -> 40.6 us (1.030)
  Pallas kernels: 35.1 us -> 36.3 us
    pallas_call x1, Pallas kernels: 35.1 us -> 36.3 us  [fast_body(): pl.pallas_call(kernel, out_shape=(jax.ShapeDtypeStruct((B, 4 * B), BF16),...]
where the time goes in v3:
time: 40.6 us; the launch traced here: 40.4 us
  Pallas kernels  36.3 us (89%)
  other arithmetic  2.18 us (5%)
  between operations  1.3 us (3%)
  local copies, waits for them, and re-layouts  0.66 us (2%)
    pallas_call x1, Pallas kernels, fast_body(): pl.pallas_call(kernel, out_shape=(jax.ShapeDtypeStruct((B, 4 * B), BF16),...  36.3 us
    broadcast_in_dim x1, other arithmetic, fast_body(): return (fgrad, wgrad.astype(F32)[None])  2.18 us

profile of v3, /device:TPU:1, one launch (start us, length us, event | category | flops | bytes accessed | tf_op | source)
XLA Modules:
  0.0 40.4 jit_solution(6485434060765704404)
XLA Ops:
  1.3 36.3 %shard_map.95 = (bf16[128,512]{1,0:T(8,128)(2,1)}, bf16[512,512]{1,0:T(8,128)(2,1)}) custom-call(bf16[128,512]{1,0:T(8,128)(2,1)} %feat_ref.1, bf16[128,512]{1,0:T(8,128)(2,1)} %grad_ref.1, bf16[512,512]{1,0:T(8,128)(2,1)} %bitcast.5, bf16[512,128]{1,0:T(8,128)(2,1)} %bitcast.6, s32[1,4]{1,0:T(1,128)} %rows_ref.1, s32[1,4]{1,0:T(1,128)} %cols_ref.1, ...), custom_call_target="tpu_custom_call" | custom-call | flops 1000000000 | bytes 4000000 | tf_op jit(solution)/shard_map/pallas_call | solution.py:274
  37.6 0.0 copy-start
  37.6 2.2 %bitcast_convert_fusion = f32[1,512,512]{2,1,0:T(8,128)} fusion(bf16[512,512]{1,0:T(8,128)(2,1)} %get-tuple-element.5), kind=kLoop, calls=%fused_computation | loop fusion | flops 262144 | bytes 1572864 | tf_op jit(solution)/shard_map/broadcast_in_dim | solution.py:314
  39.8 0.0 copy-done
  39.8 0.7 %copy.12 = bf16[128,512]{1,0:T(8,128)(2,1)} copy(bf16[128,512]{1,0:T(8,128)(2,1)S(1)} %copy-done) | data formatting | bytes 262144
Async XLA Ops:
  37.6 2.2 %copy-start = (bf16[128,512]{1,0:T(8,128)(2,1)S(1)}, bf16[128,512]{1,0:T(8,128)(2,1)}, u32[]{:S(2)}) copy-start(bf16[128,512]{1,0:T(8,128)(2,1)} %get-tuple-element.8) | copy-start | bytes 393220

commit v4 on v2

--- a/solution.py
+++ b/solution.py
@@ -47,8 +47,15 @@
     barrier = pltpu.get_barrier_semaphore()
     for j in (1, 2, 3):
         pl.semaphore_signal(barrier, inc=1, device_id={"dst": peer[j]}, device_id_type=MESH)
-        pl.semaphore_signal(barrier, inc=1, device_id={"src": zpos(j)}, device_id_type=MESH)
     pl.semaphore_signal(barrier, inc=1, device_id={"rel": 1 - r}, device_id_type=MESH)
+
+    @pl.when(s < 3)
+    def _():
+        pl.semaphore_signal(barrier, inc=1, device_id={"src": zpos(1)}, device_id_type=MESH)
+
+    @pl.when(s > 0)
+    def _():
+        pl.semaphore_signal(barrier, inc=1, device_id={"src": zpos(3)}, device_id_type=MESH)
 
     loads[0].wait()
     loads[1].wait()
@@ -67,7 +74,18 @@
     loads[5].wait()
     loads[6].wait()
 
-    pl.semaphore_wait(barrier, 7)
+    pl.semaphore_wait(barrier, 4 + (s + 3) // 4 + (6 - s) // 4)
+
+    def densify(j):
+        for k in range(4):
+            for c in range(4):
+                total = None
+                for t in range(4):
+                    code = meta[j, 4 * B + t : 4 * B + t + 1, :].astype(F32)
+                    hit = jnp.where(code == (k * 4 + peer[c]).astype(F32), 1.0, 0.0).astype(BF16)
+                    term = meta[j, t * B : (t + 1) * B, :] * hit
+                    total = term if total is None else total + term
+                dense[k, c * B : (c + 1) * B, j * B : (j + 1) * B] = total
 
     sent = []
 
@@ -91,8 +109,8 @@
         def _():
             chain(s, j, False).start()
 
-    def forward(n):
-        for j in range(4):
+    def forward(n, *js):
+        for j in js:
             @pl.when(s >= n)
             def _():
                 chain(zpos(4 - n), j, True).wait_recv()
@@ -120,22 +138,12 @@
     feat_k = go(to(feats.at[0], feats.at[1], f_send.at[1], f_recv.at[1], dst=peer[1]))
     slab_k.wait_recv()
     push(1)
+    densify(0)
     slab_y.wait_recv()
     push(2)
     slab_g.wait_recv()
     push(3)
 
-    def densify(j):
-        for k in range(4):
-            for c in range(4):
-                total = None
-                for t in range(4):
-                    code = meta[j, 4 * B + t : 4 * B + t + 1, :].astype(F32)
-                    hit = jnp.where(code == (k * 4 + peer[c]).astype(F32), 1.0, 0.0).astype(BF16)
-                    term = meta[j, t * B : (t + 1) * B, :] * hit
-                    total = term if total is None else total + term
-                dense[k, c * B : (c + 1) * B, j * B : (j + 1) * B] = total
-
     def add(at):
         total[...] += jnp.dot(dense[at], scal[at].reshape(4 * B, B), preferred_element_type=F32)
 
@@ -148,14 +156,14 @@
         def _():
             add(zpos(n))
 
-    densify(0)
+    forward(1, 0, 1)
     tile_k.wait_recv()
     densify(1)
-    forward(1)
+    forward(1, 2, 3)
     tile_y.wait_recv()
     tile_g = go(to(meta.at[2], meta.at[3], t_send.at[3], t_recv.at[3], dst=peer[1]))
     densify(2)
-    forward(2)
+    forward(2, 0, 1, 2, 3)
     tile_g.wait_recv()
     densify(3)
     feat_y.wait_recv()
@@ -169,15 +177,10 @@
     add_all(2)
     feat_g.wait_recv()
     feats_t[:, :, 3 * B :] = feats[3].T.reshape(4, B, B)
-    forward(3)
+    forward(3, 0, 1, 2, 3)
     add_all(3)
     for c in range(4):
         red[c] = total[c * B : (c + 1) * B, :]
-    rows_f32[d] = red[0]
-    rows = [
-        go(to(red.at[j], rows_f32.at[d], r_send.at[j], r_recv.at[j], dst=peer[j]))
-        for j in (1, 2, 3)
-    ]
     high, low = split_high_low(total[...])
     parts = {}
     for j in (2, 1, 3, 0):
@@ -187,6 +190,11 @@
         )
         if j:
             parts[j] = go(to(wpart.at[j], wrecv.at[j], d_send.at[j], d_recv.at[j], src=zpos(j)))
+    rows_f32[d] = red[0]
+    rows = [
+        go(to(red.at[j], rows_f32.at[d], r_send.at[j], r_recv.at[j], dst=peer[j]))
+        for j in (1, 2, 3)
+    ]
     for copy in rows:
         copy.wait_recv()
     loads[7].wait()

time: 39.4 us -> 38.5 us (0.977)
  Pallas kernels: 35.1 us -> 34.2 us
    pallas_call x1, Pallas kernels: 35.1 us -> 34.2 us  [fast_body(): pl.pallas_call(kernel, out_shape=(jax.ShapeDtypeStruct((B, 4 * B), BF16),...]
where the time goes in v4:
time: 38.5 us; the launch traced here: 38.3 us
  Pallas kernels  34.2 us (89%)
  other arithmetic  2.18 us (6%)
  between operations  1.3 us (3%)
  local copies, waits for them, and re-layouts  0.66 us (2%)
    pallas_call x1, Pallas kernels, fast_body(): pl.pallas_call(kernel, out_shape=(jax.ShapeDtypeStruct((B, 4 * B), BF16),...  34.2 us
    broadcast_in_dim x1, other arithmetic, fast_body(): return (fgrad, wgrad.astype(F32)[None])  2.18 us

profile of v4, /device:TPU:1, one launch (start us, length us, event | category | flops | bytes accessed | tf_op | source)
XLA Modules:
  0.0 38.3 jit_solution(16492890574929559898)
XLA Ops:
  1.3 34.2 %shard_map.95 = (bf16[128,512]{1,0:T(8,128)(2,1)}, bf16[512,512]{1,0:T(8,128)(2,1)}) custom-call(bf16[128,512]{1,0:T(8,128)(2,1)} %feat_ref.1, bf16[128,512]{1,0:T(8,128)(2,1)} %grad_ref.1, bf16[512,512]{1,0:T(8,128)(2,1)} %bitcast.5, bf16[512,128]{1,0:T(8,128)(2,1)} %bitcast.6, s32[1,4]{1,0:T(1,128)} %rows_ref.1, s32[1,4]{1,0:T(1,128)} %cols_ref.1, ...), custom_call_target="tpu_custom_call" | custom-call | flops 1000000000 | bytes 4000000 | tf_op jit(solution)/shard_map/pallas_call | solution.py:254
  35.4 0.0 copy-start
  35.5 2.2 %bitcast_convert_fusion = f32[1,512,512]{2,1,0:T(8,128)} fusion(bf16[512,512]{1,0:T(8,128)(2,1)} %get-tuple-element.5), kind=kLoop, calls=%fused_computation | loop fusion | flops 262144 | bytes 1572864 | tf_op jit(solution)/shard_map/broadcast_in_dim | solution.py:292
  37.6 0.0 copy-done
  37.6 0.7 %copy.12 = bf16[128,512]{1,0:T(8,128)(2,1)} copy(bf16[128,512]{1,0:T(8,128)(2,1)S(1)} %copy-done) | data formatting | bytes 262144
Async XLA Ops:
  35.4 2.2 %copy-start = (bf16[128,512]{1,0:T(8,128)(2,1)S(1)}, bf16[128,512]{1,0:T(8,128)(2,1)}, u32[]{:S(2)}) copy-start(bf16[128,512]{1,0:T(8,128)(2,1)} %get-tuple-element.8) | copy-start | bytes 393220

commit v5 on v4

--- a/solution.py
+++ b/solution.py
@@ -230,11 +230,19 @@
         gs.append(go(to(at, at, g_send.at[j], g_recv.at[j], dst=peer[1])))
     swap.wait_recv()
     fgrad_ref[...] = (mine[...] + other[...]).astype(BF16)
-    for copy in ks + gs:
+    def lay_out(slab):
+        at = pl.ds(pl.multiple_of(slab * B, B), B)
+        for q in range(4):
+            wgrad_ref[q * B : (q + 1) * B, at] = final[slab, q]
+
+    lay_out(d)
+    lay_out(peer[2])
+    for copy in ks:
         copy.wait_recv()
-    for slab in range(4):
-        for q in range(4):
-            wgrad_ref[q * B : (q + 1) * B, slab * B : (slab + 1) * B] = final[slab, q]
+    lay_out(peer[1])
+    for copy in gs:
+        copy.wait_recv()
+    lay_out(peer[3])
     for copy in sent:
         copy.wait_send()
     for n in range(3):

time: 38.5 us -> 38.4 us (level)
  no operation moved by 1% of the time
where the time goes in v5:
time: 38.4 us; the launch traced here: 38.2 us
  Pallas kernels  34.1 us (89%)
  other arithmetic  2.18 us (6%)
  between operations  1.3 us (3%)
  local copies, waits for them, and re-layouts  0.66 us (2%)
    pallas_call x1, Pallas kernels, fast_body(): pl.pallas_call(kernel, out_shape=(jax.ShapeDtypeStruct((B, 4 * B), BF16),...  34.1 us
    broadcast_in_dim x1, other arithmetic, fast_body(): return (fgrad, wgrad.astype(F32)[None])  2.18 us

profile of v5, /device:TPU:1, one launch (start us, length us, event | category | flops | bytes accessed | tf_op | source)
XLA Modules:
  0.0 38.2 jit_solution(17964443835507356074)
XLA Ops:
  1.3 34.1 %shard_map.95 = (bf16[128,512]{1,0:T(8,128)(2,1)}, bf16[512,512]{1,0:T(8,128)(2,1)}) custom-call(bf16[128,512]{1,0:T(8,128)(2,1)} %feat_ref.1, bf16[128,512]{1,0:T(8,128)(2,1)} %grad_ref.1, bf16[512,512]{1,0:T(8,128)(2,1)} %bitcast.5, bf16[512,128]{1,0:T(8,128)(2,1)} %bitcast.6, s32[1,4]{1,0:T(1,128)} %rows_ref.1, s32[1,4]{1,0:T(1,128)} %cols_ref.1, ...), custom_call_target="tpu_custom_call" | custom-call | flops 1000000000 | bytes 4000000 | tf_op jit(solution)/shard_map/pallas_call | solution.py:262
  35.4 0.0 copy-start
  35.4 2.2 %bitcast_convert_fusion = f32[1,512,512]{2,1,0:T(8,128)} fusion(bf16[512,512]{1,0:T(8,128)(2,1)} %get-tuple-element.5), kind=kLoop, calls=%fused_computation | loop fusion | flops 262144 | bytes 1572864 | tf_op jit(solution)/shard_map/broadcast_in_dim | solution.py:300
  37.6 0.0 copy-done
  37.6 0.7 %copy.12 = bf16[128,512]{1,0:T(8,128)(2,1)} copy(bf16[128,512]{1,0:T(8,128)(2,1)S(1)} %copy-done) | data formatting | bytes 262144
Async XLA Ops:
  35.4 2.2 %copy-start = (bf16[128,512]{1,0:T(8,128)(2,1)S(1)}, bf16[128,512]{1,0:T(8,128)(2,1)}, u32[]{:S(2)}) copy-start(bf16[128,512]{1,0:T(8,128)(2,1)} %get-tuple-element.8) | copy-start | bytes 393220
